TPU v7x, 32 devices: a whole 2x2x4 slice. The times are simulated.
32 devices in a mesh: group: 4 (over y, core), dev: 8 (over z, x).
Axes of the slice: x: 2, y: 2, z: 4, core: 2. Of those that a mesh axis runs over, the one named last changes fastest.
Arguments:
- node_state: bfloat16 [16384, 512], P(('group', 'dev')), may hold values from -6 to 6
- hub_state: bfloat16 [64, 512], P('dev'), may hold values from -6 to 6
- w_edge_in: bfloat16 [512, 256], replicated, may hold values from -0.25 to 0.25
- w_edge_out: bfloat16 [256, 512], replicated, may hold values from -0.375 to 0.375
- w_update: bfloat16 [512, 512], replicated, may hold values from -0.25 to 0.25
- edge_src: int32 [131072], P(('group', 'dev')), may hold values from 0 to 319
- edge_dst: int32 [131072], P(('group', 'dev')), may hold values from 0 to 319
- edge_mask: int32 [131072], P(('group', 'dev')), may hold values 0 or 1
- send_list: int32 [32, 8, 32], P(('group', 'dev')), may hold values from 0 to 511
- send_count: int32 [32, 8], P(('group', 'dev')), may hold values from 8 to 32, as said below
- node_cot: bfloat16 [16384, 512], P(('group', 'dev')), may hold values from -0.059814453 to 0.059814453
- hub_cot: bfloat16 [64, 512], P('dev'), may hold values from -0.059814453 to 0.059814453
Outputs:
- new_state: bfloat16 [16384, 512], P(('group', 'dev'))
- new_hub: bfloat16 [64, 512], P('dev')
- grad_in: float32 [512, 256], replicated
- grad_out: float32 [256, 512], replicated
- grad_update: float32 [512, 512], replicated
Inputs may be any that keep to these rules, and one draw needn't show every extreme that they name: Device 0 sends 32 live slots to peer 0: send_count[0, 0] = 32.
All inputs are finite; a program needn't handle non-finite values. No bound on the sum of `edge_mask` on one device may be relied on, other than what follows from the above.
Results may differ from a plain program's by a relative error of at most 0.0064.
The roundings to bfloat16 on the way count: a program that leaves them out, or rounds other values in their place, can miss the bound.
Values may be sent and summed in bfloat16 or wider, within the bound.
No kernel may reach another device: no remote copies, remote signals or barrier semaphores. Data moves between devices by JAX's collectives and lax.ppermute only.
A program may use at most 64 MiB of HBM per device.

v0:
```python
import jax
import jax.numpy as jnp
from jax import lax
from jax.sharding import PartitionSpec as P


def silu_grad(values):
    sigmoid_v = jax.nn.sigmoid(values)
    return sigmoid_v * (1.0 + values * (1.0 - sigmoid_v))


def finish(states, summed, degree, w_update):
    mean_part = summed / jnp.maximum(degree, 1.0)[:, None]
    mixed_rows = (states.astype(jnp.float32) + mean_part).astype(jnp.bfloat16)
    pre_update = jnp.dot(mixed_rows, w_update, preferred_element_type=jnp.float32)
    updated = (states.astype(jnp.float32) + jax.nn.silu(pre_update)).astype(jnp.bfloat16)
    return (mixed_rows, pre_update, updated)


def backward_rows(cotangent, pre_update, degree, w_update):
    grad_pre = (cotangent.astype(jnp.float32) * silu_grad(pre_update)).astype(jnp.bfloat16)
    grad_mix = jnp.dot(grad_pre, w_update.T, preferred_element_type=jnp.float32)
    grad_sum = (grad_mix / jnp.maximum(degree, 1.0)[:, None]).astype(jnp.bfloat16)
    return (grad_pre, grad_sum)


def shards(
    node_state,
    hub_state,
    w_edge_in,
    w_edge_out,
    w_update,
    edge_src,
    edge_dst,
    edge_mask,
    send_list,
    send_count,
    node_cot,
    hub_cot,
):
    width = node_state.shape[1]
    master_rows = node_state.shape[0]
    send_rows = send_list[0]
    peer_total = send_rows.shape[0]
    slot_width = send_rows.shape[1]
    mirror_total = peer_total * slot_width
    live_slot = jnp.arange(slot_width)[None, :] < send_count[0][:, None]
    flat_rows = send_rows.reshape(-1)
    flat_live = live_slot.reshape(-1)
    selector = (
        (flat_rows[:, None] == jnp.arange(master_rows)[None, :]) & flat_live[:, None]
    ).astype(jnp.bfloat16)
    contract = (((0,), (0,)), ((), ()))
    outgoing = jnp.dot(selector, node_state, preferred_element_type=jnp.float32).astype(
        jnp.bfloat16
    )
    mirror_rows = lax.all_to_all(
        outgoing.reshape(peer_total, slot_width, width),
        "dev",
        split_axis=0,
        concat_axis=0,
        tiled=True,
    )
    hub_table = lax.all_gather(hub_state, "dev", axis=0, tiled=True)
    local_table = jnp.concatenate([mirror_rows.reshape(mirror_total, width), hub_table], axis=0)
    local_rows = local_table.shape[0]
    edge_total = edge_src.shape[0]
    block_size = min(1024, edge_total)
    block_count = edge_total // block_size
    sources = edge_src.reshape(block_count, block_size)
    targets = edge_dst.reshape(block_count, block_size)
    edge_keep = edge_mask.reshape(block_count, block_size)
    row_ids = jnp.arange(local_rows)[None, :]

    def forward_step(totals, pieces):
        source_ids, target_ids, keep_ids = pieces
        gathered = local_table[source_ids]
        pre_act = jnp.dot(gathered, w_edge_in, preferred_element_type=jnp.float32)
        hidden = jax.nn.silu(pre_act).astype(jnp.bfloat16)
        message = jnp.dot(hidden, w_edge_out, preferred_element_type=jnp.float32).astype(
            jnp.bfloat16
        )
        onehot = ((target_ids[:, None] == row_ids) & (keep_ids[:, None] > 0)).astype(jnp.bfloat16)
        added = lax.dot_general(onehot, message, contract, preferred_element_type=jnp.float32)
        tally = jnp.sum(onehot, axis=0, dtype=jnp.float32)
        return ((totals[0] + added, totals[1] + tally), pre_act)

    start_fwd = (jnp.zeros((local_rows, width), jnp.float32), jnp.zeros((local_rows,), jnp.float32))
    (partial_value, counts_local), saved_acts = lax.scan(
        forward_step, start_fwd, (sources, targets, edge_keep)
    )
    mirror_part = (
        partial_value[:mirror_total].reshape(peer_total, slot_width, width).astype(jnp.bfloat16)
    )
    mirror_count = counts_local[:mirror_total].reshape(peer_total, slot_width).astype(jnp.bfloat16)
    back_part, back_count = (
        lax.all_to_all(mirror_part, "dev", split_axis=0, concat_axis=0, tiled=True),
        lax.all_to_all(mirror_count, "dev", split_axis=0, concat_axis=0, tiled=True),
    )
    summed = lax.dot_general(
        selector,
        back_part.reshape(mirror_total, width),
        contract,
        preferred_element_type=jnp.float32,
    )
    degree = lax.dot_general(
        selector, back_count.reshape(mirror_total, 1), contract, preferred_element_type=jnp.float32
    )[:, 0]
    hub_part = partial_value[mirror_total:]
    hub_count = counts_local[mirror_total:]
    whole_part, whole_count = (
        lax.psum(hub_part.astype(jnp.bfloat16), "group").astype(jnp.float32),
        lax.psum(hub_count.astype(jnp.bfloat16), "group").astype(jnp.float32),
    )
    hub_summed, hub_degree = (
        lax.psum_scatter(
            whole_part.astype(jnp.bfloat16), "dev", scatter_dimension=0, tiled=True
        ).astype(jnp.float32),
        lax.psum_scatter(
            whole_count.astype(jnp.bfloat16), "dev", scatter_dimension=0, tiled=True
        ).astype(jnp.float32),
    )
    mixed_rows, pre_update, new_state = finish(node_state, summed, degree, w_update)
    hub_mixed, hub_pre, new_hub = finish(hub_state, hub_summed, hub_degree, w_update)
    grad_pre, grad_sum = backward_rows(node_cot, pre_update, degree, w_update)
    hub_grad_pre, hub_grad_sum = backward_rows(hub_cot, hub_pre, hub_degree, w_update)
    grad_outgoing = jnp.dot(selector, grad_sum, preferred_element_type=jnp.float32).astype(
        jnp.bfloat16
    )
    grad_mirror = lax.all_to_all(
        grad_outgoing.reshape(peer_total, slot_width, width),
        "dev",
        split_axis=0,
        concat_axis=0,
        tiled=True,
    )
    grad_hubs = lax.all_gather(hub_grad_sum, "dev", axis=0, tiled=True)
    grad_table = jnp.concatenate([grad_mirror.reshape(mirror_total, width), grad_hubs], axis=0)
    hub_weight = (lax.axis_index("group") == 0).astype(jnp.float32)
    grad_update = lax.dot_general(
        mixed_rows, grad_pre, contract, preferred_element_type=jnp.float32
    )
    grad_update = grad_update + hub_weight * lax.dot_general(
        hub_mixed, hub_grad_pre, contract, preferred_element_type=jnp.float32
    )

    def backward_step(totals, pieces):
        source_ids, target_ids, keep_ids, pre_act = pieces
        gathered = local_table[source_ids]
        hidden = jax.nn.silu(pre_act).astype(jnp.bfloat16)
        grad_message = jnp.where(
            keep_ids[:, None] > 0, grad_table[target_ids], jnp.zeros((), jnp.bfloat16)
        )
        grad_w_out = lax.dot_general(
            hidden, grad_message, contract, preferred_element_type=jnp.float32
        )
        grad_hidden = jnp.dot(grad_message, w_edge_out.T, preferred_element_type=jnp.float32)
        grad_act = (grad_hidden * silu_grad(pre_act)).astype(jnp.bfloat16)
        grad_w_in = lax.dot_general(
            gathered, grad_act, contract, preferred_element_type=jnp.float32
        )
        return ((totals[0] + grad_w_in, totals[1] + grad_w_out), None)

    start = (jnp.zeros(w_edge_in.shape, jnp.float32), jnp.zeros(w_edge_out.shape, jnp.float32))
    local_grads, _ = lax.scan(backward_step, start, (sources, targets, edge_keep, saved_acts))
    grad_in, grad_out, grad_upd = lax.psum(
        (local_grads[0], local_grads[1], grad_update), ("group", "dev")
    )
    return (new_state, new_hub, grad_in, grad_out, grad_upd)


def solution(mesh):
    return jax.shard_map(
        shards,
        mesh=mesh,
        in_specs=(
            P(("group", "dev"), None),
            P("dev", None),
            P(),
            P(),
            P(),
            P(("group", "dev")),
            P(("group", "dev")),
            P(("group", "dev")),
            P(("group", "dev"), None, None),
            P(("group", "dev"), None),
            P(("group", "dev"), None),
            P("dev", None),
        ),
        out_specs=(P(("group", "dev"), None), P("dev", None), P(), P(), P()),
        check_vma=False,
    )
```

profile of v0, /device:TPU:0, one launch (start us, length us, event | category | flops | bytes accessed | tf_op | source)
XLA Modules:
  0.0 417.0 jit_solution(8544541724577750692)
XLA Ops:
  7.2 0.8 iota_compare_fusion.2
  8.1 0.8 eq.35
  8.8 2.1 convolution_convert_fusion.1
  10.9 7.2 %all-to-all-start = ((bf16[8,32,512]{2,1,0:T(8,128)(2,1)}), bf16[8,32,512]{2,1,0:T(8,128)(2,1)S(1)}, u32[]{:S(2)}, u32[]{:S(2)}) async-start(bf16[8,32,512]{2,1,0:T(8,128)(2,1)} %bitcast.1), calls=%async_computation | async-start | bytes 524288 | tf_op jit(solution)/shard_map/all_to_all | solution.py:57
  18.2 0.7 reshape.192
  18.9 0.7 reshape.193
  19.7 0.7 reshape.194
  20.4 31.2 %all_gather.6 = bf16[64,512]{1,0:T(8,128)(2,1)S(1)} all-gather(bf16[8,512]{1,0:T(8,128)(2,1)} %param.17), channel_id=1, replica_groups=mesh['group'=4,'dev'=8] {'dev'}, dimensions={0}, use_global_device_ids=true | all-gather | bytes 73728 | tf_op jit(solution)/shard_map/all_gather | solution.py:64
  51.7 33.4 %while.28 = (s32[]{:T(128)}, f32[320,512]{1,0:T(8,128)}, f32[320]{0:T(512)S(1)}, f32[4,1024,256]{2,1,0:T(8,128)}, s32[4,1024]{1,0:T(4,128)S(1)}, /*index=5*/s32[...) while((s32[]{:T(128)}, f32[320,512]{1,0:T(8,128)}, ...), condition=%wide.region_2.3_spmd.clone, body=%wide.region_0.2_spmd.clone.sunk | while | flops 876877120 | bytes 10273476 | solution.py:89
  51.8 4.0 gather_fusion
  55.7 1.4 bitcast_dynamic-update-slice_fusion.2
  57.2 1.7 fusion.93
  58.9 0.3 convert_reduce_fusion.2
  59.3 4.0 gather_fusion
  63.3 1.5 bitcast_dynamic-update-slice_fusion.2
  64.8 2.7 fusion.93
  67.5 0.3 convert_reduce_fusion.2
  67.9 4.0 gather_fusion
  71.9 1.4 bitcast_dynamic-update-slice_fusion.2
  73.4 2.7 fusion.93
  76.1 0.3 convert_reduce_fusion.2
  76.5 4.0 gather_fusion
  80.5 1.4 bitcast_dynamic-update-slice_fusion.2
  82.0 2.7 fusion.93
  85.1 0.7 convert_element_type.118
  85.8 5.4 %all-to-all-start.2 = ((bf16[8,1,32]{2,1,0:T(2,128)(2,1)}), bf16[8,1,32]{2,1,0:T(2,128)(2,1)S(1)}, u32[]{:S(2)}, u32[]{:S(2)}) async-start(bf16[8,1,32]{2,1,0:T(2,128)(2,1)} %convert_element_type.118), calls=%async_computation.2 | async-start | bytes 8192 | tf_op jit(solution)/shard_map/all_to_all | solution.py:98
  91.3 0.6 dynamic-slice
  92.5 1.2 convert.8
  93.7 0.7 slice.34
  94.5 0.6 slice.35
  95.1 21.8 %all-reduce = bf16[64]{0:T(256)(128)(2,1)S(1)} all-reduce(bf16[64]{0:T(256)(128)(2,1)S(1)} %slice.27), channel_id=3, replica_groups=mesh['group'=4,'dev'=8] {'dev'}, use_global_device_ids=true, to_apply=%region_6.7.clone | all-reduce | flops 64 | bytes 256
  117.0 3.4 all-to-all-start.1
  120.8 38.2 %reduce-scatter.2.cloned.1.call-done = bf16[8,512]{1,0:T(8,128)(2,1)} async-done(((bf16[64,512]{1,0:T(8,128)(2,1)}), bf16[8,512]{1,0:T(8,128)(2,1)}) %reduce-scatter.2.cloned.1.call-update) | async-done | bytes 8208 | tf_op jit(solution)/shard_map/reduce_scatter | solution.py:116
  159.0 6.0 %all-reduce.2 = (bf16[8,512]{1,0:T(8,128)(2,1)S(1)}, bf16[8]{0:T(256)(128)(2,1)S(1)}) all-reduce(bf16[8,512]{1,0:T(8,128)(2,1)} %reduce-scatter.2.cloned.1.call-done, bf16[8]{0:T(256)(128)(2,1)S(1)} %dynamic-slice.1), channel_id=1, replica_groups=mesh['group'=4,'dev'=8] {'group'}, use_global_device_ids=true, to_apply=%region_3.4 | all-reduce | flops 4104 | bytes 16416 | tf_op jit(solution)/shard_map/psum | solution.py:112
  165.0 0.8 fusion.60
  166.1 30.5 %all_gather.7 = bf16[64,512]{1,0:T(8,128)(2,1)S(1)} all-gather(bf16[8,512]{1,0:T(8,128)(2,1)S(1)} %fusion.42), channel_id=1, replica_groups=mesh['group'=4,'dev'=8] {'dev'}, dimensions={0}, use_global_device_ids=true | all-gather | bytes 73728 | tf_op jit(solution)/shard_map/all_gather | solution.py:137
  196.6 1.5 fusion.38
  198.2 2.7 multiply_convert_fusion.3
  200.9 1.4 fusion.41
  202.3 3.6 all-to-all-start.3
  205.9 0.5 fusion.64
  206.4 1.4 fusion.36
  207.8 6.3 %all-to-all-done.3 = bf16[8,32,512]{2,1,0:T(8,128)(2,1)S(1)} async-done(((bf16[8,32,512]{2,1,0:T(8,128)(2,1)}), bf16[8,32,512]{2,1,0:T(8,128)(2,1)S(1)}, u32[]{:S(2)}, u32[]{:S(2)}) %all-to-all-start.3) | async-done | bytes 262176 | tf_op jit(solution)/shard_map/all_to_all | solution.py:130
  214.1 56.7 %while.29 = (s32[]{:T(128)}, f32[512,256]{1,0:T(8,128)}, f32[256,512]{1,0:T(8,128)}, s32[4,1024]{1,0:T(4,128)S(1)}, bf16[320,512]{1,0:T(8,128)(2,1)S(1)}, /*inde...) while((s32[]{:T(128)}, f32[512,256]{1,0:T(8,128)}, ...), condition=%wide.region_8.9_spmd.clone, body=%wide.region_7.8_spmd.clone.sunk | while | flops 810558464 | bytes 11845768 | solution.py:165
  214.2 4.0 gather_fusion.2
  218.2 4.0 gather_fusion.1
  222.2 3.3 convolution_add_fusion.4
  225.5 2.6 convolution_add_fusion.5
  228.1 4.0 gather_fusion.2
  232.1 4.0 gather_fusion.1
  236.1 3.4 convolution_add_fusion.4
  239.6 2.8 convolution_add_fusion.5
  242.4 4.0 gather_fusion.2
  246.3 4.0 gather_fusion.1
  250.4 3.4 convolution_add_fusion.4
  253.8 2.8 convolution_add_fusion.5
  256.6 4.0 gather_fusion.2
  260.6 4.0 gather_fusion.1
  264.6 3.4 convolution_add_fusion.4
  268.0 2.7 convolution_add_fusion.5
  270.8 133.3 %all-reduce.5.cloned.1.call-done = (f32[512,256]{1,0:T(8,128)}, f32[256,512]{1,0:T(8,128)}, f32[512,512]{1,0:T(8,128)}) async-done(((f32[512,256]{1,0:T(8,128)}, f32[256,512]{1,0:T(8,128)}, f32[512,512]{1,0:T(8,128)}), (f32[512,256]{1,0:T(8,128)}, f32[256,512]{1,0:T(8,128)}, f32[512,512]{1,0:T(8,128)})) %all-reduce.5.cloned.1.call-update) | async-done | bytes 2097168 | tf_op jit(solution)/shard_map/psum | solution.py:166
  404.1 1.9 copy.44
  406.0 1.9 copy.45
  407.9 2.3 copy.46
  (88 shorter events, 1.9 us)
Async XLA Ops:
  7.2 157.8 %copy-start = (bf16[512,512]{1,0:T(8,128)(2,1)S(1)}, bf16[512,512]{1,0:T(8,128)(2,1)}, u32[]{:S(2)}) copy-start(bf16[512,512]{1,0:T(8,128)(2,1)} %param.20) | copy-start | bytes 1572868
  10.9 40.7 %all-to-all-start = ((bf16[8,32,512]{2,1,0:T(8,128)(2,1)}), bf16[8,32,512]{2,1,0:T(8,128)(2,1)S(1)}, u32[]{:S(2)}, u32[]{:S(2)}) async-start(bf16[8,32,512]{2,1,0:T(8,128)(2,1)} %bitcast.1), calls=%async_computation | async-start | bytes 524288 | tf_op jit(solution)/shard_map/all_to_all | solution.py:57
  51.7 39.6 %copy-start.6 = (u32[32]{0:T(128)S(1)}, u32[32]{0:T(128)}, u32[]{:S(2)}) copy-start(u32[32]{0:T(128)} %constant.65) | copy-start | bytes 388
  51.7 113.3 %copy-start.2 = (bf16[8,512]{1,0:T(8,128)(2,1)S(1)}, bf16[8,512]{1,0:T(8,128)(2,1)}, u32[]{:S(2)}) copy-start(bf16[8,512]{1,0:T(8,128)(2,1)} %param.17) | copy-start | bytes 24580
  51.7 114.2 %copy-start.3 = (bf16[8,512]{1,0:T(8,128)(2,1)S(1)}, bf16[8,512]{1,0:T(8,128)(2,1)}, u32[]{:S(2)}) copy-start(bf16[8,512]{1,0:T(8,128)(2,1)} %param.27) | copy-start | bytes 24580
  51.7 4.0 copy-start.1
  51.8 5.5 %copy-start.5 = (bf16[256,512]{1,0:T(8,128)(2,1)S(1)}, bf16[256,512]{1,0:T(8,128)(2,1)}, u32[]{:S(2)}) copy-start(bf16[256,512]{1,0:T(8,128)(2,1)} %get-tuple-element.406) | copy-start | bytes 786436 | tf_op jit(solution)/shard_map/while
  59.2 4.0 copy-start.1
  59.3 5.5 %copy-start.5 = (bf16[256,512]{1,0:T(8,128)(2,1)S(1)}, bf16[256,512]{1,0:T(8,128)(2,1)}, u32[]{:S(2)}) copy-start(bf16[256,512]{1,0:T(8,128)(2,1)} %get-tuple-element.406) | copy-start | bytes 786436 | tf_op jit(solution)/shard_map/while
  67.9 4.0 copy-start.1
  67.9 5.5 %copy-start.5 = (bf16[256,512]{1,0:T(8,128)(2,1)S(1)}, bf16[256,512]{1,0:T(8,128)(2,1)}, u32[]{:S(2)}) copy-start(bf16[256,512]{1,0:T(8,128)(2,1)} %get-tuple-element.406) | copy-start | bytes 786436 | tf_op jit(solution)/shard_map/while
  76.5 4.0 copy-start.1
  76.5 5.5 %copy-start.5 = (bf16[256,512]{1,0:T(8,128)(2,1)S(1)}, bf16[256,512]{1,0:T(8,128)(2,1)}, u32[]{:S(2)}) copy-start(bf16[256,512]{1,0:T(8,128)(2,1)} %get-tuple-element.406) | copy-start | bytes 786436 | tf_op jit(solution)/shard_map/while
  85.8 31.2 %all-to-all-start.2 = ((bf16[8,1,32]{2,1,0:T(2,128)(2,1)}), bf16[8,1,32]{2,1,0:T(2,128)(2,1)S(1)}, u32[]{:S(2)}, u32[]{:S(2)}) async-start(bf16[8,1,32]{2,1,0:T(2,128)(2,1)} %convert_element_type.118), calls=%async_computation.2 | async-start | bytes 8192 | tf_op jit(solution)/shard_map/all_to_all | solution.py:98
  91.2 67.8 %reduce-scatter.2.cloned.1.call-start = ((), (), s32[]{:S(2)}) async-start(), calls=%async_computation.5 | async-start | bytes 73728 | tf_op jit(solution)/shard_map/reduce_scatter | solution.py:116
  92.5 105.6 %copy-start.4 = (bf16[512,512]{1,0:T(8,128)(2,1)S(1)}, bf16[512,512]{1,0:T(8,128)(2,1)}, u32[]{:S(2)}) copy-start(bf16[512,512]{1,0:T(8,128)(2,1)} %param.26) | copy-start | bytes 1572868
  117.0 79.6 %all-to-all-start.1 = ((bf16[8,32,512]{2,1,0:T(8,128)(2,1)}), bf16[8,32,512]{2,1,0:T(8,128)(2,1)S(1)}, u32[]{:S(2)}, u32[]{:S(2)}) async-start(bf16[8,32,512]{2,1,0:T(8,128)(2,1)} %bitcast.3), calls=%async_computation.1 | async-start | bytes 524288 | tf_op jit(solution)/shard_map/all_to_all | solution.py:97
  202.3 11.8 %all-to-all-start.3 = ((bf16[8,32,512]{2,1,0:T(8,128)(2,1)}), bf16[8,32,512]{2,1,0:T(8,128)(2,1)S(1)}, u32[]{:S(2)}, u32[]{:S(2)}) async-start(bf16[8,32,512]{2,1,0:T(8,128)(2,1)} %bitcast.6), calls=%async_computation.3 | async-start | bytes 524288 | tf_op jit(solution)/shard_map/all_to_all | solution.py:130
  205.9 198.3 %all-reduce.5.cloned.1.call-start = ((), (), s32[]{:S(2)}) async-start(), calls=%async_computation.6 | async-start | bytes 4194304 | tf_op jit(solution)/shard_map/psum | solution.py:166
Sparse Core Ops, SparseCore 0:
  96.0 62.9 reduce-scatter.1
  270.9 133.1 all-reduce.4
where the time goes:
time: 418 us; the launch traced here: 417 us
  waiting for transfers between devices  178 us (43%)
  blocking collectives  89.5 us (21%)
  local copies, waits for them, and re-layouts  59.5 us (14%)
  matrix products  51.1 us (12%)
  starting transfers between devices  19.8 us (5%)
  between operations  14.9 us (4%)
    psum x1, waiting for transfers between devices, shards(): lax.psum((local_grads[0], local_grads[1], grad_update), ('group', 'dev'))  133 us
    reduce_scatter x1, waiting for transfers between devices, shards(): lax.psum_scatter(whole_part.astype(jnp.bfloat16), 'dev', scatter_dimensio...  38.2 us
    all_gather x1, blocking collectives, shards(): hub_table = lax.all_gather(hub_state, 'dev', axis=0, tiled=True)  31.2 us
    all_gather x1, blocking collectives, shards(): grad_hubs = lax.all_gather(hub_grad_sum, 'dev', axis=0, tiled=True)  30.5 us
    unnamed x1, blocking collectives  21.8 us
    gather x4, local copies, waits for them, and re-layouts, backward_step(): grad_table[target_ids]  15.9 us
    gather x4, local copies, waits for them, and re-layouts, backward_step(): gathered = local_table[source_ids]  15.9 us
    gather x4, local copies, waits for them, and re-layouts, forward_step(): gathered = local_table[source_ids]  15.9 us
  transfers between devices with their start and end apart: 6, of which 3 were waited for; matrix products, arithmetic and copies ran while one was open for 2% of the time, Pallas kernels for 0%

commit v1 on v0

--- a/solution.py
+++ b/solution.py
@@ -127,13 +127,16 @@
     grad_outgoing = jnp.dot(selector, grad_sum, preferred_element_type=jnp.float32).astype(
         jnp.bfloat16
     )
-    grad_mirror = lax.all_to_all(
-        grad_outgoing.reshape(peer_total, slot_width, width),
-        "dev",
-        split_axis=0,
-        concat_axis=0,
-        tiled=True,
-    )
+    value = grad_outgoing.reshape(peer_total, slot_width, width)
+    ways, here = (lax.axis_size("dev"), lax.axis_index("dev"))
+    width_2 = value.shape[0] // ways
+    turned = jnp.roll(value, -here * width_2, axis=0)
+    got = [lax.slice_in_dim(turned, 0, width_2, axis=0)]
+    for far in range(1, ways):
+        sent = lax.slice_in_dim(turned, far * width_2, (far + 1) * width_2, axis=0)
+        got.append(lax.ppermute(sent, "dev", [(d, (d + far) % ways) for d in range(ways)]))
+    line = jnp.concatenate(got[::-1], axis=0)
+    grad_mirror = jnp.roll(line, (here + 1) * got[0].shape[0], axis=0)
     grad_hubs = lax.all_gather(hub_grad_sum, "dev", axis=0, tiled=True)
     grad_table = jnp.concatenate([grad_mirror.reshape(mirror_total, width), grad_hubs], axis=0)
     hub_weight = (lax.axis_index("group") == 0).astype(jnp.float32)

time: 418 us -> 422 us (level)
  starting transfers between devices: 19.8 us -> 25 us
    ppermute x0 -> x7, starting transfers between devices: none -> 8.8 us  [shards(): lax.ppermute(sent, 'dev', [(d, (d + far) % ways) for d in range(ways)])]
    all_to_all x1 -> x0, waiting for transfers between devices: 6.32 us -> none  [shards(): lax.all_to_all(grad_outgoing.reshape(peer_total, slot_width, width), 'dev...]
    ppermute x0 -> x7, waiting for transfers between devices: none -> 5.11 us  [shards(): lax.ppermute(sent, 'dev', [(d, (d + far) % ways) for d in range(ways)])]
  transfers between devices with their start and end apart: 6 -> 12, of which waited for: 3 -> 5; matrix products, arithmetic and copies ran while one was open for 2% -> 2% of each run, Pallas kernels for 0% -> 0%
where the time goes in v1:
time: 422 us; the launch traced here: 421 us
  waiting for transfers between devices  177 us (42%)
  blocking collectives  89.5 us (21%)
  local copies, waits for them, and re-layouts  59.6 us (14%)
  matrix products  50.4 us (12%)
  starting transfers between devices  25 us (6%)
  between operations  15 us (4%)
    psum x1, waiting for transfers between devices, shards(): lax.psum((local_grads[0], local_grads[1], grad_update), ('group', 'dev'))  134 us
    reduce_scatter x1, waiting for transfers between devices, shards(): lax.psum_scatter(whole_part.astype(jnp.bfloat16), 'dev', scatter_dimensio...  38.2 us
    all_gather x1, blocking collectives, shards(): hub_table = lax.all_gather(hub_state, 'dev', axis=0, tiled=True)  31.2 us
    all_gather x1, blocking collectives, shards(): grad_hubs = lax.all_gather(hub_grad_sum, 'dev', axis=0, tiled=True)  30.5 us
    unnamed x1, blocking collectives  21.8 us
    gather x4, local copies, waits for them, and re-layouts, forward_step(): gathered = local_table[source_ids]  15.9 us
    gather x4, local copies, waits for them, and re-layouts, backward_step(): grad_table[target_ids]  15.9 us
    gather x4, local copies, waits for them, and re-layouts, backward_step(): gathered = local_table[source_ids]  15.9 us
  transfers between devices with their start and end apart: 12, of which 5 were waited for; matrix products, arithmetic and copies ran while one was open for 2% of the time, Pallas kernels for 0%

profile of v1, /device:TPU:0, one launch (start us, length us, event | category | flops | bytes accessed | tf_op | source)
XLA Modules:
  0.0 420.9 jit_solution(12386570361111681003)
XLA Ops:
  7.2 0.8 iota_compare_fusion.2
  8.1 0.8 eq.37
  8.8 2.1 convolution_convert_fusion.1
  10.9 7.2 %all-to-all-start = ((bf16[8,32,512]{2,1,0:T(8,128)(2,1)}), bf16[8,32,512]{2,1,0:T(8,128)(2,1)S(1)}, u32[]{:S(2)}, u32[]{:S(2)}) async-start(bf16[8,32,512]{2,1,0:T(8,128)(2,1)} %bitcast.1), calls=%async_computation | async-start | bytes 524288 | tf_op jit(solution)/shard_map/all_to_all | solution.py:57
  18.2 0.7 reshape.192
  19.0 0.7 reshape.193
  19.7 0.7 reshape.194
  20.4 31.2 %all_gather.6 = bf16[64,512]{1,0:T(8,128)(2,1)S(1)} all-gather(bf16[8,512]{1,0:T(8,128)(2,1)} %param.19), channel_id=1, replica_groups=mesh['group'=4,'dev'=8] {'dev'}, dimensions={0}, use_global_device_ids=true | all-gather | bytes 73728 | tf_op jit(solution)/shard_map/all_gather | solution.py:64
  51.7 33.3 %while.28 = (s32[]{:T(128)}, f32[320,512]{1,0:T(8,128)}, f32[320]{0:T(512)S(1)}, f32[4,1024,256]{2,1,0:T(8,128)}, s32[4,1024]{1,0:T(4,128)S(1)}, /*index=5*/s32[...) while((s32[]{:T(128)}, f32[320,512]{1,0:T(8,128)}, ...), condition=%wide.region_2.3_spmd.clone, body=%wide.region_0.2_spmd.clone.sunk | while | flops 876877120 | bytes 10273476 | solution.py:89
  51.8 4.0 gather_fusion
  55.7 1.4 bitcast_dynamic-update-slice_fusion.2
  57.2 1.7 fusion.96
  59.3 4.0 gather_fusion
  63.3 1.4 bitcast_dynamic-update-slice_fusion.2
  64.8 2.7 fusion.96
  67.9 4.0 gather_fusion
  71.9 1.4 bitcast_dynamic-update-slice_fusion.2
  73.3 2.7 fusion.96
  76.5 4.0 gather_fusion
  80.5 1.4 bitcast_dynamic-update-slice_fusion.2
  82.0 2.7 fusion.96
  85.1 0.7 convert_element_type.118
  85.7 5.4 %all-to-all-start.2 = ((bf16[8,1,32]{2,1,0:T(2,128)(2,1)}), bf16[8,1,32]{2,1,0:T(2,128)(2,1)S(1)}, u32[]{:S(2)}, u32[]{:S(2)}) async-start(bf16[8,1,32]{2,1,0:T(2,128)(2,1)} %convert_element_type.118), calls=%async_computation.2 | async-start | bytes 8192 | tf_op jit(solution)/shard_map/all_to_all | solution.py:98
  92.5 1.2 convert.8
  93.7 0.7 slice.66
  94.4 0.6 slice.67
  95.1 21.8 %all-reduce = bf16[64]{0:T(256)(128)(2,1)S(1)} all-reduce(bf16[64]{0:T(256)(128)(2,1)S(1)} %slice.51), channel_id=3, replica_groups=mesh['group'=4,'dev'=8] {'dev'}, use_global_device_ids=true, to_apply=%region_6.7.clone | all-reduce | flops 64 | bytes 256
  117.0 3.4 all-to-all-start.1
  120.8 38.2 %reduce-scatter.2.cloned.1.call-done = bf16[8,512]{1,0:T(8,128)(2,1)} async-done(((bf16[64,512]{1,0:T(8,128)(2,1)}), bf16[8,512]{1,0:T(8,128)(2,1)}) %reduce-scatter.2.cloned.1.call-update) | async-done | bytes 8208 | tf_op jit(solution)/shard_map/reduce_scatter | solution.py:116
  159.0 6.0 %all-reduce.2 = (bf16[8,512]{1,0:T(8,128)(2,1)S(1)}, bf16[8]{0:T(256)(128)(2,1)S(1)}) all-reduce(bf16[8,512]{1,0:T(8,128)(2,1)} %reduce-scatter.2.cloned.1.call-done, bf16[8]{0:T(256)(128)(2,1)S(1)} %dynamic-slice.1), channel_id=1, replica_groups=mesh['group'=4,'dev'=8] {'group'}, use_global_device_ids=true, to_apply=%region_3.4 | all-reduce | flops 4104 | bytes 16416 | tf_op jit(solution)/shard_map/psum | solution.py:112
  165.0 0.8 fusion.62
  166.1 30.5 %all_gather.7 = bf16[64,512]{1,0:T(8,128)(2,1)S(1)} all-gather(bf16[8,512]{1,0:T(8,128)(2,1)S(1)} %fusion.42), channel_id=1, replica_groups=mesh['group'=4,'dev'=8] {'dev'}, dimensions={0}, use_global_device_ids=true | all-gather | bytes 73728 | tf_op jit(solution)/shard_map/all_gather | solution.py:140
  196.6 1.5 fusion.38
  198.1 2.7 multiply_convert_fusion.3
  201.3 0.7 fusion.41
  202.2 2.4 collective-permute-start
  204.6 3.0 collective-permute-start.3
  207.7 1.4 fusion.36
  209.1 1.8 collective-permute-start.5
  210.9 1.5 collective-permute-start.6
  212.4 0.9 collective-permute-done.4
  213.3 2.8 collective-permute-done.5
  216.1 1.5 collective-permute-done.6
  217.7 56.7 %while.29 = (s32[]{:T(128)}, f32[512,256]{1,0:T(8,128)}, f32[256,512]{1,0:T(8,128)}, s32[4,1024]{1,0:T(4,128)S(1)}, bf16[320,512]{1,0:T(8,128)(2,1)S(1)}, /*inde...) while((s32[]{:T(128)}, f32[512,256]{1,0:T(8,128)}, ...), condition=%wide.region_8.10_spmd.clone, body=%wide.region_7.9_spmd.clone.sunk | while | flops 810558464 | bytes 11845768 | solution.py:168
  217.7 4.0 gather_fusion.2
  221.7 4.0 gather_fusion.1
  225.7 3.3 convolution_add_fusion.4
  229.0 2.6 convolution_add_fusion.5
  231.7 4.0 gather_fusion.2
  235.7 4.0 gather_fusion.1
  239.7 3.4 convolution_add_fusion.4
  243.1 2.8 convolution_add_fusion.5
  245.9 4.0 gather_fusion.2
  249.9 4.0 gather_fusion.1
  253.9 3.4 convolution_add_fusion.4
  257.4 2.7 convolution_add_fusion.5
  260.1 4.0 gather_fusion.2
  264.1 4.0 gather_fusion.1
  268.1 3.4 convolution_add_fusion.4
  271.6 2.8 convolution_add_fusion.5
  274.4 133.7 %all-reduce.5.cloned.1.call-done = (f32[512,256]{1,0:T(8,128)}, f32[256,512]{1,0:T(8,128)}, f32[512,512]{1,0:T(8,128)}) async-done(((f32[512,256]{1,0:T(8,128)}, f32[256,512]{1,0:T(8,128)}, f32[512,512]{1,0:T(8,128)}), (f32[512,256]{1,0:T(8,128)}, f32[256,512]{1,0:T(8,128)}, f32[512,512]{1,0:T(8,128)})) %all-reduce.5.cloned.1.call-update) | async-done | bytes 2097168 | tf_op jit(solution)/shard_map/psum | solution.py:169
  408.1 1.9 copy.51
  410.0 1.9 copy.52
  411.8 2.3 copy.53
  (111 shorter events, 4.3 us)
Async XLA Ops:
  7.2 157.8 %copy-start = (bf16[512,512]{1,0:T(8,128)(2,1)S(1)}, bf16[512,512]{1,0:T(8,128)(2,1)}, u32[]{:S(2)}) copy-start(bf16[512,512]{1,0:T(8,128)(2,1)} %param.22) | copy-start | bytes 1572868
  10.9 40.7 %all-to-all-start = ((bf16[8,32,512]{2,1,0:T(8,128)(2,1)}), bf16[8,32,512]{2,1,0:T(8,128)(2,1)S(1)}, u32[]{:S(2)}, u32[]{:S(2)}) async-start(bf16[8,32,512]{2,1,0:T(8,128)(2,1)} %bitcast.1), calls=%async_computation | async-start | bytes 524288 | tf_op jit(solution)/shard_map/all_to_all | solution.py:57
  51.7 39.6 %copy-start.6 = (u32[32]{0:T(128)S(1)}, u32[32]{0:T(128)}, u32[]{:S(2)}) copy-start(u32[32]{0:T(128)} %constant.87) | copy-start | bytes 388
  51.7 113.3 %copy-start.2 = (bf16[8,512]{1,0:T(8,128)(2,1)S(1)}, bf16[8,512]{1,0:T(8,128)(2,1)}, u32[]{:S(2)}) copy-start(bf16[8,512]{1,0:T(8,128)(2,1)} %param.19) | copy-start | bytes 24580
  51.7 114.2 %copy-start.3 = (bf16[8,512]{1,0:T(8,128)(2,1)S(1)}, bf16[8,512]{1,0:T(8,128)(2,1)}, u32[]{:S(2)}) copy-start(bf16[8,512]{1,0:T(8,128)(2,1)} %param.29) | copy-start | bytes 24580
  51.7 4.0 copy-start.1
  51.8 5.5 %copy-start.5 = (bf16[256,512]{1,0:T(8,128)(2,1)S(1)}, bf16[256,512]{1,0:T(8,128)(2,1)}, u32[]{:S(2)}) copy-start(bf16[256,512]{1,0:T(8,128)(2,1)} %get-tuple-element.414) | copy-start | bytes 786436 | tf_op jit(solution)/shard_map/while
  59.2 4.0 copy-start.1
  59.3 5.5 %copy-start.5 = (bf16[256,512]{1,0:T(8,128)(2,1)S(1)}, bf16[256,512]{1,0:T(8,128)(2,1)}, u32[]{:S(2)}) copy-start(bf16[256,512]{1,0:T(8,128)(2,1)} %get-tuple-element.414) | copy-start | bytes 786436 | tf_op jit(solution)/shard_map/while
  67.9 4.0 copy-start.1
  67.9 5.5 %copy-start.5 = (bf16[256,512]{1,0:T(8,128)(2,1)S(1)}, bf16[256,512]{1,0:T(8,128)(2,1)}, u32[]{:S(2)}) copy-start(bf16[256,512]{1,0:T(8,128)(2,1)} %get-tuple-element.414) | copy-start | bytes 786436 | tf_op jit(solution)/shard_map/while
  76.5 4.0 copy-start.1
  76.5 5.5 %copy-start.5 = (bf16[256,512]{1,0:T(8,128)(2,1)S(1)}, bf16[256,512]{1,0:T(8,128)(2,1)}, u32[]{:S(2)}) copy-start(bf16[256,512]{1,0:T(8,128)(2,1)} %get-tuple-element.414) | copy-start | bytes 786436 | tf_op jit(solution)/shard_map/while
  85.7 31.2 %all-to-all-start.2 = ((bf16[8,1,32]{2,1,0:T(2,128)(2,1)}), bf16[8,1,32]{2,1,0:T(2,128)(2,1)S(1)}, u32[]{:S(2)}, u32[]{:S(2)}) async-start(bf16[8,1,32]{2,1,0:T(2,128)(2,1)} %convert_element_type.118), calls=%async_computation.2 | async-start | bytes 8192 | tf_op jit(solution)/shard_map/all_to_all | solution.py:98
  91.2 67.8 %reduce-scatter.2.cloned.1.call-start = ((), (), s32[]{:S(2)}) async-start(), calls=%async_computation.4 | async-start | bytes 73728 | tf_op jit(solution)/shard_map/reduce_scatter | solution.py:116
  92.5 105.7 %copy-start.4 = (bf16[512,512]{1,0:T(8,128)(2,1)S(1)}, bf16[512,512]{1,0:T(8,128)(2,1)}, u32[]{:S(2)}) copy-start(bf16[512,512]{1,0:T(8,128)(2,1)} %param.28) | copy-start | bytes 1572868
  117.0 79.6 %all-to-all-start.1 = ((bf16[8,32,512]{2,1,0:T(8,128)(2,1)}), bf16[8,32,512]{2,1,0:T(8,128)(2,1)S(1)}, u32[]{:S(2)}, u32[]{:S(2)}) async-start(bf16[8,32,512]{2,1,0:T(8,128)(2,1)} %bitcast.3), calls=%async_computation.1 | async-start | bytes 524288 | tf_op jit(solution)/shard_map/all_to_all | solution.py:97
  120.4 287.7 %all-reduce.5.cloned.1.call-start = ((), (), s32[]{:S(2)}) async-start(), calls=%async_computation.5 | async-start | bytes 4194304 | tf_op jit(solution)/shard_map/psum | solution.py:169
  202.2 6.9 %collective-permute-start = (bf16[1,32,512]{2,1,0:T(8,128)(2,1)S(1)}, bf16[1,32,512]{2,1,0:T(8,128)(2,1)S(1)}, u32[]{:S(2)}, u32[]{:S(2)}) collective-permute-start(bf16[1,32,512]{2,1,0:T(8,128)(2,1)S(1)} %get-tuple-element.248), channel_id=1, source_target_pairs={{0,7},{1,0},{2,1},{3,2},{4,3},{5,4},{6,5},{7,6},{8,15},{9,8},{10,9... | collective-permute-start | bytes 98312 | tf_op jit(solution)/shard_map/ppermute | solution.py:137
  204.6 6.4 %collective-permute-start.1 = (bf16[1,32,512]{2,1,0:T(8,128)(2,1)S(1)}, bf16[1,32,512]{2,1,0:T(8,128)(2,1)S(1)}, u32[]{:S(2)}, u32[]{:S(2)}) collective-permute-start(bf16[1,32,512]{2,1,0:T(8,128)(2,1)S(1)} %get-tuple-element.247), channel_id=1, source_target_pairs={{0,6},{1,7},{2,0},{3,1},{4,2},{5,3},{6,4},{7,5},{8,14},{9,15},{10,... | collective-permute-start | bytes 98312 | tf_op jit(solution)/shard_map/ppermute | solution.py:137
  204.6 7.8 %collective-permute-start.2 = (bf16[1,32,512]{2,1,0:T(8,128)(2,1)S(1)}, bf16[1,32,512]{2,1,0:T(8,128)(2,1)S(1)}, u32[]{:S(2)}, u32[]{:S(2)}) collective-permute-start(bf16[1,32,512]{2,1,0:T(8,128)(2,1)S(1)} %get-tuple-element.246), channel_id=1, source_target_pairs={{0,5},{1,6},{2,7},{3,0},{4,1},{5,2},{6,3},{7,4},{8,13},{9,14},{10,... | collective-permute-start | bytes 98312 | tf_op jit(solution)/shard_map/ppermute | solution.py:137
  204.6 7.8 %collective-permute-start.3 = (bf16[1,32,512]{2,1,0:T(8,128)(2,1)S(1)}, bf16[1,32,512]{2,1,0:T(8,128)(2,1)S(1)}, u32[]{:S(2)}, u32[]{:S(2)}) collective-permute-start(bf16[1,32,512]{2,1,0:T(8,128)(2,1)S(1)} %get-tuple-element.245), channel_id=1, source_target_pairs={{0,4},{1,5},{2,6},{3,7},{4,0},{5,1},{6,2},{7,3},{8,12},{9,13},{10,... | collective-permute-start | bytes 98312 | tf_op jit(solution)/shard_map/ppermute | solution.py:137
  207.5 5.7 %collective-permute-start.4 = (bf16[1,32,512]{2,1,0:T(8,128)(2,1)S(1)}, bf16[1,32,512]{2,1,0:T(8,128)(2,1)S(1)}, u32[]{:S(2)}, u32[]{:S(2)}) collective-permute-start(bf16[1,32,512]{2,1,0:T(8,128)(2,1)S(1)} %get-tuple-element.244), channel_id=1, source_target_pairs={{0,3},{1,4},{2,5},{3,6},{4,7},{5,0},{6,1},{7,2},{8,11},{9,12},{10,... | collective-permute-start | bytes 98312 | tf_op jit(solution)/shard_map/ppermute | solution.py:137
  209.1 6.9 %collective-permute-start.5 = (bf16[1,32,512]{2,1,0:T(8,128)(2,1)S(1)}, bf16[1,32,512]{2,1,0:T(8,128)(2,1)S(1)}, u32[]{:S(2)}, u32[]{:S(2)}) collective-permute-start(bf16[1,32,512]{2,1,0:T(8,128)(2,1)S(1)} %get-tuple-element.243), channel_id=1, source_target_pairs={{0,2},{1,3},{2,4},{3,5},{4,6},{5,7},{6,0},{7,1},{8,10},{9,11},{10,... | collective-permute-start | bytes 98312 | tf_op jit(solution)/shard_map/ppermute | solution.py:137
  210.9 6.6 %collective-permute-start.6 = (bf16[1,32,512]{2,1,0:T(8,128)(2,1)S(1)}, bf16[1,32,512]{2,1,0:T(8,128)(2,1)S(1)}, u32[]{:S(2)}, u32[]{:S(2)}) collective-permute-start(bf16[1,32,512]{2,1,0:T(8,128)(2,1)S(1)} %get-tuple-element.242), channel_id=1, source_target_pairs={{0,1},{1,2},{2,3},{3,4},{4,5},{5,6},{6,7},{7,0},{8,9},{9,10},{10,1... | collective-permute-start | bytes 98312 | tf_op jit(solution)/shard_map/ppermute | solution.py:137
Sparse Core Ops, SparseCore 0:
  96.0 62.9 reduce-scatter.1
  274.5 133.5 all-reduce.4
